TPU v7x, 32 devices: a whole 2x2x4 slice. The times are simulated.
32 devices in a mesh: src: 4 (over x, core), tgt: 4 (over z), feat: 2 (over y).
Axes of the slice: x: 2, y: 2, z: 4, core: 2. Of those that a mesh axis runs over, the one named last changes fastest.
Arguments:
- activations: bfloat16 [4, 1792, 1280], P('src', None, 'feat'), may hold values from 0 to 12, as said below
- window_ids: int32 [4, 640], replicated, may hold values from 0 to 1279, as said below
- decoders: bfloat16 [4, 4, 640, 2048], P('src', 'tgt', 'feat'), may hold values from -3 to 3
- encoders: bfloat16 [4, 2048, 640], P('tgt', ('src', 'feat')), may hold values from -0.125 to 0.125
Outputs:
- weighted: float32 [4, 4, 640, 640], P('src', 'tgt', 'feat')
Inputs may be any that keep to these rules, and one draw needn't show every extreme that they name: `window_ids`: each layer's list names 640 distinct features. activations are zero or positive.
All inputs are finite; a program needn't handle non-finite values.
Results may differ from a plain program's by a relative error of at most 0.0029.
Values may be sent and summed in bfloat16 or wider, within the bound.
A program may use at most 64 MiB of HBM per device.

v0:
```python
import jax
import jax.numpy as jnp
from jax import lax
from jax.sharding import PartitionSpec as P


def broadcast(array, axis, root):
    mine = lax.axis_index(axis) == root
    return lax.psum(jnp.where(mine, array, jnp.zeros_like(array)), axis)


def per_device(activations, window_ids, decoders, encoders):
    source = lax.axis_index("src")
    block_index = lax.axis_index("tgt")
    feat_index = lax.axis_index("feat")
    target_count = decoders.shape[1]
    slice_width = decoders.shape[2]
    local_feats = activations.shape[2]
    token_count = activations.shape[1]
    own_ids = lax.dynamic_index_in_dim(window_ids, source, 0, keepdims=False)
    local_cols = own_ids - feat_index * local_feats
    inside = (local_cols >= 0) & (local_cols < local_feats)
    picked = jnp.take(activations[0], jnp.clip(local_cols, 0, local_feats - 1), axis=1)
    picked = jnp.where(inside[None, :], picked, jnp.zeros_like(picked))
    summed = lax.psum(picked, "feat").astype(jnp.float32)
    own_window = summed.astype(jnp.bfloat16)
    own_slice = lax.dynamic_slice_in_dim(own_window, feat_index * slice_width, slice_width, 1)
    inner_product_matrices = []
    for offset in range(target_count):
        target = block_index * target_count + offset
        target_cols = broadcast(own_slice, "src", target)
        product = lax.dot_general(
            own_window, target_cols, (((0,), (0,)), ((), ())), preferred_element_type=jnp.float32
        )
        inner_product_matrices.append(product / token_count)
    stacked_inner_products = jnp.stack(inner_product_matrices)
    coactive = lax.all_to_all(
        stacked_inner_products, "feat", split_axis=1, concat_axis=2, tiled=True
    )
    depth_numbers = block_index * target_count + jnp.arange(target_count)
    live_mask = (depth_numbers >= source).astype(jnp.float32)
    written = decoders[0].astype(jnp.float32) * live_mask[:, None, None]
    running = jnp.cumsum(written, 0)
    before = jnp.concatenate([jnp.zeros_like(running[:1]), running[:-1]], 0)
    block_total = running[-1]
    all_totals = lax.all_gather(block_total[None], "tgt", axis=0, tiled=True)
    lower_mask = (jnp.arange(all_totals.shape[0]) < block_index).astype(jnp.float32)
    earlier = jnp.sum(all_totals * lower_mask[:, None, None], 0)
    leading_sum = (earlier[None] + before).astype(jnp.bfloat16)
    row_block = lax.all_gather(encoders, "feat", axis=1, tiled=True)
    virtual = jnp.einsum(
        "kid,kdj->kij",
        leading_sum,
        lax.all_gather(row_block, "src", axis=1, tiled=True),
        preferred_element_type=jnp.float32,
    )
    return (virtual * coactive)[None]


def solution(mesh):
    in_specs = (
        P("src", None, "feat"),
        P(),
        P("src", "tgt", "feat", None),
        P("tgt", ("src", "feat"), None),
    )
    out_specs = P("src", "tgt", "feat", None)
    return jax.shard_map(
        per_device, mesh=mesh, in_specs=in_specs, out_specs=out_specs, check_vma=False
    )
```

profile of v0, /device:TPU:29, one launch (start us, length us, event | category | flops | bytes accessed | tf_op | source)
XLA Modules:
  0.0 313.5 jit_solution(16002437869022353614)
XLA Ops:
  7.4 0.0 all-reduce.3.cloned.1.call-start
  7.4 0.7 fusion.15
  8.1 0.7 clamp_reduce_fusion
  8.8 0.7 and_reduce_fusion
  9.6 3.1 copy.9
  12.7 3.9 %gather_fusion = bf16[640,1792]{1,0:T(8,128)(2,1)} fusion(bf16[1792,640]{0,1:T(8,128)(2,1)S(1)} %bitcast.27, s32[1024]{0:T(1024)S(1)} %pad_clamp_fusion), kind=kCustom, calls=%fused_computation | custom fusion | bytes 4590080 | tf_op jit(solution)/shard_map/jit(_take)/gather | solution.py:23
  16.6 3.4 %select_bitcast_fusion = bf16[1792,640]{0,1:T(8,128)(2,1)} fusion(bf16[640,1792]{1,0:T(8,128)(2,1)} %gather_fusion, pred[640]{0:T(1024)(128)(4,1)S(1)} %and_reduce_fusion, pred[640]{0:T(1024)(128)(4,1)S(1)} %compare_and_fusion), kind=kLoop, calls=%fused_computation.6 | loop fusion | flops 2293760 | bytes 4588800 | tf_op jit(solution)/shard_map/jit(_where)/select_n | solution.py:24
  20.0 0.0 all-reduce.3.cloned.1.call-update
  20.0 0.0 copy-start
  20.0 0.0 all-reduce.5.cloned.1.call-start
  20.1 67.3 %all-reduce.3.cloned.1.call-done = bf16[1792,640]{0,1:T(8,128)(2,1)} async-done(((bf16[1792,640]{0,1:T(8,128)(2,1)}), bf16[1792,640]{0,1:T(8,128)(2,1)}) %all-reduce.3.cloned.1.call-update) | async-done | bytes 2293776 | tf_op jit(solution)/shard_map/psum | solution.py:25
  87.4 2.5 dynamic-slice_select_fusion
  89.9 0.0 all-reduce.5.cloned.1.call-update
  89.9 0.0 all-gather.6.cloned.1.call-start
  89.9 0.0 copy-done
  89.9 1.8 convert_multiply_fusion
  91.7 0.0 copy-start.2
  91.7 0.0 copy-start.1
  91.7 0.0 all-gather.6.cloned.1.call-update
  91.8 0.0 all-gather.4.cloned.1.call-start
  91.8 0.9 copy-done.2
  92.7 9.3 %all_gather.10 = bf16[1,512,640]{2,1,0:T(8,128)(2,1)} all-gather(bf16[1,256,640]{2,1,0:T(8,128)(2,1)S(1)} %copy-done.2), channel_id=1, replica_groups=mesh['src'=4,'tgt'=4,'feat'=2] {'feat'}, dimensions={1}, use_global_device_ids=true | all-gather | bytes 983040 | tf_op jit(solution)/shard_map/all_gather | solution.py:50
  102.1 0.0 all-gather.4.cloned.1.call-update
  102.1 25.8 %all-reduce.5.cloned.1.call-done = bf16[1792,320]{0,1:T(8,128)(2,1)} async-done(((bf16[1792,320]{0,1:T(8,128)(2,1)}), bf16[1792,320]{0,1:T(8,128)(2,1)}) %all-reduce.5.cloned.1.call-update) | async-done | bytes 1146896 | tf_op jit(solution)/shard_map/psum | solution.py:9
  127.9 0.0 copy-done.1
  127.9 2.4 fusion.14
  130.2 1.9 copy.10
  132.2 3.8 %all-to-all-start = ((f32[1,640,320]{2,0,1:T(1,128)}), f32[1,640,320]{2,0,1:T(1,128)S(1)}, u32[]{:S(2)}, u32[]{:S(2)}) async-start(f32[1,640,320]{2,0,1:T(1,128)} %copy.10), calls=%async_computation | async-start | bytes 1966080 | tf_op jit(solution)/shard_map/all_to_all | solution.py:37
  136.0 11.1 %all-to-all-done = f32[1,640,320]{2,0,1:T(1,128)S(1)} async-done(((f32[1,640,320]{2,0,1:T(1,128)}), f32[1,640,320]{2,0,1:T(1,128)S(1)}, u32[]{:S(2)}, u32[]{:S(2)}) %all-to-all-start) | async-done | bytes 819232 | tf_op jit(solution)/shard_map/all_to_all | solution.py:37
  147.2 0.8 copy.13
  147.9 0.7 all_to_all.16
  148.6 125.5 %all-gather.6.cloned.1.call-done = f32[4,1,320,2048]{3,2,1,0:T(8,128)} async-done(((f32[1,1,320,2048]{3,2,1,0:T(8,128)}), f32[4,1,320,2048]{3,2,1,0:T(8,128)}) %all-gather.6.cloned.1.call-update) | async-done | bytes 10485776 | tf_op jit(solution)/shard_map/all_gather | solution.py:46
  274.1 5.4 %fusion = bf16[320,2048]{1,0:T(8,128)(2,1)S(1)} fusion(f32[4,1,320,2048]{3,2,1,0:T(8,128)} %all-gather.6.cloned.1.call-done, f32[4]{0:T(128)S(1)} %compare_convert_fusion), kind=kLoop, calls=%fused_computation.2 | loop fusion | flops 4587520 | bytes 11796496 | tf_op jit(solution)/shard_map/reduce_sum | solution.py:48
  279.5 22.7 %all-gather.4.cloned.1.call-done = bf16[1,2048,640]{2,1,0:T(8,128)(2,1)} async-done(((bf16[1,512,640]{2,1,0:T(8,128)(2,1)}), bf16[1,2048,640]{2,1,0:T(8,128)(2,1)}) %all-gather.4.cloned.1.call-update) | async-done | bytes 2621456 | tf_op jit(solution)/shard_map/all_gather | solution.py:54
  302.2 3.8 %fusion.9 = f32[1,1,320,640]{3,2,1,0:T(8,128)} fusion(f32[320,640]{1,0:T(8,128)S(1)} %all_to_all.16, bf16[1,2048,640]{2,1,0:T(8,128)(2,1)} %all-gather.4.cloned.1.call-done, bf16[320,2048]{1,0:T(8,128)(2,1)S(1)} %fusion), kind=kOutput, calls=%fused_computation.9 | convolution fusion | flops 839065600 | bytes 5570560 | tf_op jit(solution)/shard_map/kid,kdj->kij/dot_general | solution.py:51
  (3 shorter events, 0.0 us)
Async XLA Ops:
  7.4 80.0 %all-reduce.3.cloned.1.call-start = ((), (), s32[]{:S(2)}) async-start(), calls=%async_computation.2 | async-start | bytes 4587520 | tf_op jit(solution)/shard_map/psum | solution.py:25
  20.0 69.9 %copy-start = (bf16[1,1,320,2048]{3,2,1,0:T(8,128)(2,1)S(1)}, bf16[1,1,320,2048]{3,2,1,0:T(8,128)(2,1)}, u32[]{:S(2)}) copy-start(bf16[1,1,320,2048]{3,2,1,0:T(8,128)(2,1)} %param.6) | copy-start | bytes 3932164
  20.0 107.9 %all-reduce.5.cloned.1.call-start = ((), (), s32[]{:S(2)}) async-start(), calls=%async_computation.3 | async-start | bytes 2293760 | tf_op jit(solution)/shard_map/psum | solution.py:9
  89.9 184.3 %all-gather.6.cloned.1.call-start = ((), (), s32[]{:S(2)}) async-start(), calls=%async_computation.4 | async-start | bytes 13107200 | tf_op jit(solution)/shard_map/all_gather | solution.py:46
  91.7 1.0 copy-start.2
  91.7 36.2 %copy-start.1 = (bf16[1792,640]{0,1:T(8,128)(2,1)S(1)}, bf16[1792,640]{0,1:T(8,128)(2,1)}, u32[]{:S(2)}) copy-start(bf16[1792,640]{0,1:T(8,128)(2,1)} %all-reduce.3.cloned.1.call-done) | copy-start | bytes 6881284
  91.8 210.5 %all-gather.4.cloned.1.call-start = ((), (), s32[]{:S(2)}) async-start(), calls=%async_computation.1 | async-start | bytes 3276800 | tf_op jit(solution)/shard_map/all_gather | solution.py:54
  132.2 15.0 %all-to-all-start = ((f32[1,640,320]{2,0,1:T(1,128)}), f32[1,640,320]{2,0,1:T(1,128)S(1)}, u32[]{:S(2)}, u32[]{:S(2)}) async-start(f32[1,640,320]{2,0,1:T(1,128)} %copy.10), calls=%async_computation | async-start | bytes 1966080 | tf_op jit(solution)/shard_map/all_to_all | solution.py:37
Sparse Core Ops, SparseCore 0:
  20.1 67.2 all-reduce.2
  90.0 37.8 all-reduce.4
Sparse Core Ops, SparseCore 1:
  92.0 182.1 all-gather.5
  275.6 26.5 all-gather.3
where the time goes:
time: 315 us; the launch traced here: 313 us
  waiting for transfers between devices  253 us (80%)
  other arithmetic  15.2 us (5%)
  between operations  14.9 us (5%)
  local copies, waits for them, and re-layouts  11.3 us (4%)
  blocking collectives  9.35 us (3%)
  matrix products  6.16 us (2%)
  starting transfers between devices  3.95 us (1%)
    all_gather x1, waiting for transfers between devices, per_device(): all_totals = lax.all_gather(block_total[None], 'tgt', axis=0, tiled=True)  126 us
    psum x1, waiting for transfers between devices, per_device(): summed = lax.psum(picked, 'feat').astype(jnp.float32)  67.3 us
    psum x1, waiting for transfers between devices, broadcast(): return lax.psum(jnp.where(mine, array, jnp.zeros_like(array)), axis)  25.8 us
    all_gather x1, waiting for transfers between devices, per_device(): lax.all_gather(row_block, 'src', axis=1, tiled=True)  22.7 us
    all_to_all x1, waiting for transfers between devices, per_device(): lax.all_to_all(stacked_inner_products, 'feat', split_axis=1, concat_axis=...  11.1 us
    all_gather x1, blocking collectives, per_device(): row_block = lax.all_gather(encoders, 'feat', axis=1, tiled=True)  9.35 us
  transfers between devices with their start and end apart: 5, of which 5 were waited for; matrix products, arithmetic and copies ran while one was open for 4% of the time, Pallas kernels for 0%

commit v1 on v0

v1 whole, which is shorter than its diff:
```python
import functools

import jax
import jax.numpy as jnp
from jax import lax
from jax.experimental import pallas as pl
from jax.experimental.pallas import tpu as pltpu
from jax.sharding import PartitionSpec as P

MESH = pl.DeviceIdType.MESH
NT = (((1,), (1,)), ((), ()))


def each(count, fn, start=0):
    if count - start <= 8:
        for i in range(start, count):
            fn(i)
    else:
        lax.fori_loop(start, count, lambda i, c: (fn(i), c)[1], 0)


def kernel(S, T, F, acts, ids, dec, enc, out, idcol, pt_send, pt_recv, w_own, w_all, e_all,
           ch_recv, ch_send, prefix, p_s, p_r, e_s, e_r, ef_s, ef_r, w_s, w_r, wf_s, wf_r,
           c_s, c_r, l_s):
    src, tgt, feat = lax.axis_index("src"), lax.axis_index("tgt"), lax.axis_index("feat")
    K, wf = dec.shape[1], dec.shape[2]
    tokens, raw = acts.shape[1], acts.shape[2]
    FW = ids.shape[1]
    half = tokens // 2
    rows = enc.shape[1]
    G = S // 2 * F
    parity = lax.rem(src, 2)
    mate = src + 1 - 2 * parity
    group = (src // 2) * F + feat
    chunk = 32 if wf % 32 == 0 else 16
    chunks = wf // chunk

    barrier = pltpu.get_barrier_semaphore()
    plane = src * F + feat

    def greet(i):
        other = lax.rem(plane + i, S * F)
        pl.semaphore_signal(barrier, inc=1, device_id=(other // F, tgt, lax.rem(other, F)),
                            device_id_type=MESH)

    each(S * F, greet, 1)

    @pl.when(tgt > 0)
    def _():
        pl.semaphore_signal(barrier, inc=1, device_id=(src, tgt - 1, feat), device_id_type=MESH)

    @pl.when(tgt < T - 1)
    def _():
        pl.semaphore_signal(barrier, inc=1, device_id=(src, tgt + 1, feat), device_id_type=MESH)

    own_ids = ids[pl.ds(src, 1), :]
    idcol[...] = jnp.transpose(jnp.broadcast_to(own_ids, (128, FW)))

    def picked(f_index, q):
        col = idcol[pl.ds(pl.multiple_of(f_index * wf, 16), wf), :][:, :1] - feat * raw
        one_hot = (col == lax.broadcasted_iota(jnp.int32, (wf, raw), 1)).astype(
            jnp.float32).astype(jnp.bfloat16)
        return lax.dot_general(one_hot, acts[0, q * half:(q + 1) * half, :], NT,
                               preferred_element_type=jnp.float32).astype(jnp.bfloat16)

    def remote(a, b, s, r, where):
        return pltpu.make_async_remote_copy(src_ref=a, dst_ref=b, send_sem=s, recv_sem=r,
                                            device_id=where, device_id_type=MESH)

    def chain_copy(i):
        at = pl.ds(pl.multiple_of(i * chunk, 16), chunk)
        return remote(ch_send.at[at], ch_recv.at[at], c_s.at[i], c_r.at[i],
                      (src, lax.rem(tgt + 1, T), feat))

    def chain(first, last):
        def step(i, carry):
            at = pl.ds(pl.multiple_of(i * chunk, 16), chunk)

            @pl.when(tgt > 0)
            def _():
                chain_copy(i).wait_recv()

            total = ch_recv[at, :].astype(jnp.float32)
            for k in range(K):
                prefix[k, at, :] = total.astype(jnp.bfloat16)
                live = (tgt * K + k >= src).astype(jnp.float32)
                total = total + dec[0, k, at, :].astype(jnp.float32) * live

            @pl.when(tgt < T - 1)
            def _():
                ch_send[at, :] = total.astype(jnp.bfloat16)
                chain_copy(i).start()
            return carry
        lax.fori_loop(first, last, step, 0)

    def e_at(p):
        return e_all.at[:, pl.ds(pl.multiple_of(p * rows, 16), rows), :]

    def e_place(j, par):
        g = lax.rem(group - j + G, G)
        return (2 * (g // F) + par) * F + lax.rem(g, F)

    def e_copy(j):
        g = lax.rem(group + j, G)
        return remote(enc, e_at(plane), e_s.at[j], e_r.at[j],
                      (2 * (g // F) + parity, tgt, lax.rem(g, F)))

    def e_own_forward():
        return remote(enc, e_at(plane), ef_s.at[0], ef_r.at[0], (mate, tgt, feat))

    def e_forward(j):
        place = e_place(j, parity)
        return remote(e_at(place), e_at(place), ef_s.at[j], ef_r.at[j], (mate, tgt, feat))

    def p_copy(q, j):
        return remote(pt_send.at[q, j - 1], pt_recv.at[q, j - 1], p_s.at[q, j - 1],
                      p_r.at[q, j - 1], (src, tgt, lax.rem(feat + j, F)))

    def w_at(q, k, f):
        return w_all.at[q, k, pl.ds(pl.multiple_of(f * wf, 16), wf), :]

    def w_copy(q, k, j):
        g = lax.rem(group + j, G)
        return remote(w_own.at[q], w_at(q, k, feat), w_s.at[q, k, j], w_r.at[k, feat],
                      (2 * (g // F) + q, tgt, lax.rem(g, F)))

    def w_arrival(k, f):
        return remote(w_own.at[0], w_at(parity, k, f), w_s.at[0, k, 0], w_r.at[k, f],
                      (mate, tgt, feat))

    def w_forward(k, f):
        return remote(w_at(parity, k, f), w_at(parity, k, f), wf_s.at[k, f], wf_r.at[k, f],
                      (mate, tgt, feat))

    def w_forward_in(k, f):
        other = w_at(1 - parity, k, f)
        return remote(other, other, wf_s.at[k, f], wf_r.at[k, f], (mate, tgt, feat))

    def if_sends(q, k, j, fn):
        owner = src == tgt * K + k
        if isinstance(j, int) and j > 0:
            pl.when(owner)(fn)
        else:
            pl.when(owner & ((j > 0) | (parity != q)))(fn)

    @pl.when(tgt == 0)
    def _():
        ch_recv[...] = jnp.zeros_like(ch_recv)

    pl.semaphore_wait(barrier, S * F - 1 + (tgt > 0).astype(jnp.int32)
                      + (tgt < T - 1).astype(jnp.int32))

    @pl.when(tgt == 0)
    def _():
        chain(0, chunks)

    for q in range(2):
        for j in range(1, F):
            pt_send[q, j - 1] = picked(lax.rem(feat + j, F), q)
            p_copy(q, j).start()

    each(G, lambda j: e_copy(j).start(), 1)
    e_own_forward().start()
    local = pltpu.make_async_copy(enc, e_at(plane), l_s)
    local.start()
    for q in range(2):
        w_own[q] = picked(feat, q)
    marks = [0, chunks * 4 // 10, chunks * 8 // 10, chunks]

    def chain_part(n):
        @pl.when(tgt > 0)
        def _():
            chain(marks[n], marks[n + 1])

    for q in range(2):
        chain_part(q)
        for j in range(1, F):
            p_copy(q, j).wait_recv()
            w_own[q] = w_own[q] + pt_recv[q, j - 1]
        for k in range(K):
            def send(j):
                if_sends(q, k, j, lambda: w_copy(q, k, j).start())
            each(G, send)

            @pl.when(src == tgt * K + k)
            def _():
                w_all[q, k, pl.ds(pl.multiple_of(feat * wf, 16), wf), :] = w_own[q]

    def pass_on(j):
        e_copy(j).wait_recv()
        e_forward(j).start()

    each(G, pass_on, 1)
    chain_part(2)

    def mine(k, f):
        return (src == tgt * K + k) & (feat == f)

    def mates(k, f):
        return (mate == tgt * K + k) & (feat == f)

    for k in range(K):
        for f in range(F):
            @pl.when(jnp.logical_not(mine(k, f)))
            def _():
                w_arrival(k, f).wait_recv()

            @pl.when(jnp.logical_not(mates(k, f)))
            def _():
                w_forward(k, f).start()

    e_own_in = lambda j: remote(e_at(e_place(j, 1 - parity)), e_at(e_place(j, 1 - parity)),
                                ef_s.at[j], ef_r.at[j], (mate, tgt, feat))
    each(G, lambda j: e_own_in(j).wait_recv())
    local.wait()
    for k in range(K):
        out[0, k] = jnp.dot(prefix[k], e_all[k], preferred_element_type=jnp.float32)

    for k in range(K):
        for f in range(F):
            @pl.when(jnp.logical_not(mine(k, f)))
            def _():
                w_forward_in(k, f).wait_recv()
        gram = lax.dot_general(w_own[0], w_all[0, k], NT, preferred_element_type=jnp.float32)
        gram += lax.dot_general(w_own[1], w_all[1, k], NT, preferred_element_type=jnp.float32)
        out[0, k] = out[0, k] * (gram / tokens)

    @pl.when(tgt < T - 1)
    def _():
        each(chunks, lambda i: chain_copy(i).wait_send())

    for q in range(2):
        for j in range(1, F):
            p_copy(q, j).wait_send()
        for k in range(K):
            def sent(j):
                if_sends(q, k, j, lambda: w_copy(q, k, j).wait_send())
            each(G, sent)
    each(G, lambda j: e_copy(j).wait_send(), 1)
    e_own_forward().wait_send()
    each(G, lambda j: e_forward(j).wait_send(), 1)
    for k in range(K):
        for f in range(F):
            @pl.when(jnp.logical_not(mates(k, f)))
            def _():
                w_forward(k, f).wait_send()


def solution(mesh):
    S, T, F = mesh.shape["src"], mesh.shape["tgt"], mesh.shape["feat"]

    def per_device(activations, window_ids, decoders, encoders):
        _, tokens, raw = activations.shape
        FW = window_ids.shape[1]
        _, K, wf, D = decoders.shape
        G = S // 2 * F
        bf = jnp.bfloat16
        dma = pltpu.SemaphoreType.DMA
        chunks = wf // (32 if wf % 32 == 0 else 16)
        vmem = pl.BlockSpec(memory_space=pltpu.VMEM)
        return pl.pallas_call(
            functools.partial(kernel, S, T, F),
            out_shape=jax.ShapeDtypeStruct((1, K, wf, FW), jnp.float32),
            in_specs=[vmem] * 4,
            out_specs=vmem,
            scratch_shapes=[
                pltpu.VMEM((FW, 128), jnp.int32),
                pltpu.VMEM((2, F - 1, wf, tokens // 2), bf),
                pltpu.VMEM((2, F - 1, wf, tokens // 2), bf),
                pltpu.VMEM((2, wf, tokens // 2), bf),
                pltpu.VMEM((2, K, FW, tokens // 2), bf),
                pltpu.VMEM((K, D, FW), bf),
                pltpu.VMEM((wf, D), bf),
                pltpu.VMEM((wf, D), bf),
                pltpu.VMEM((K, wf, D), bf),
                dma((2, F - 1)), dma((2, F - 1)),
                dma((G,)), dma((G,)), dma((G,)), dma((G,)),
                dma((2, K, G)), dma((K, F)), dma((K, F)), dma((K, F)),
                dma((chunks,)), dma((chunks,)), dma(()),
            ],
            compiler_params=pltpu.CompilerParams(
                collective_id=0, has_side_effects=True, vmem_limit_bytes=56 * 2**20),
        )(activations, window_ids, decoders, encoders)

    in_specs = (
        P("src", None, "feat"),
        P(),
        P("src", "tgt", "feat", None),
        P("tgt", ("src", "feat"), None),
    )
    return jax.shard_map(
        per_device, mesh=mesh, in_specs=in_specs, out_specs=P("src", "tgt", "feat", None),
        check_vma=False,
    )
```

time: 315 us -> 75.3 us (0.24)
  the two profiles are of different devices: /device:TPU:29 before, /device:TPU:31 now
where the time goes in v1:
time: 75.3 us; the launch traced here: 75.1 us
  Pallas kernels  73 us (97%)
  local copies, waits for them, and re-layouts  2.09 us (3%)
    pallas_call x1, Pallas kernels, per_device(): pl.pallas_call(functools.partial(kernel, S, T, F), out_shape=jax.ShapeDty...  73 us
    unnamed x1, local copies, waits for them, and re-layouts  2.09 us

profile of v1, /device:TPU:31, one launch (start us, length us, event | category | flops | bytes accessed | tf_op | source)
XLA Modules:
  0.0 75.1 jit_solution(11098033068046846104)
XLA Ops:
  0.0 73.0 %shard_map.46 = f32[1,1,320,640]{3,2,1,0:T(8,128)} custom-call(bf16[1,1792,640]{2,1,0:T(8,128)(2,1)} %acts.1, s32[4,640]{1,0:T(4,128)} %ids.1, bf16[1,1,320,2048]{3,2,1,0:T(8,128)(2,1)} %dec.1, bf16[1,256,640]{2,1,0:T(8,128)(2,1)} %enc.1), custom_call_target="tpu_custom_call" | custom-call | tf_op jit(solution)/shard_map/pallas_call | solution.py:261
  73.0 2.1 %copy.6 = f32[1,1,320,640]{3,2,1,0:T(8,128)} copy(f32[1,1,320,640]{3,2,1,0:T(8,128)} %shard_map.46) | data formatting | bytes 1638400

commit v2 on v1

--- a/solution.py
+++ b/solution.py
@@ -20,7 +20,7 @@
 
 
 def kernel(S, T, F, acts, ids, dec, enc, out, idcol, pt_send, pt_recv, w_own, w_all, e_all,
-           ch_recv, ch_send, prefix, p_s, p_r, e_s, e_r, ef_s, ef_r, w_s, w_r, wf_s, wf_r,
+           ch_recv, ch_send, prefix, p_s, p_r, z_s, z_r, ey_s, ey_r, ex_s, ex_r, ef_s, ef_r, w_s, w_r, wf_s, wf_r,
            c_s, c_r, l_s):
     src, tgt, feat = lax.axis_index("src"), lax.axis_index("tgt"), lax.axis_index("feat")
     K, wf = dec.shape[1], dec.shape[2]
@@ -34,6 +34,12 @@
     group = (src // 2) * F + feat
     chunk = 32 if wf % 32 == 0 else 16
     chunks = wf // chunk
+    pieces = 2 if wf % 32 == 0 else 1
+    part = wf // pieces
+    early = lax.rem(tgt, 2)
+    late = 1 - early
+    H = S // 2
+    side = src // 2
 
     barrier = pltpu.get_barrier_semaphore()
     plane = src * F + feat
@@ -56,11 +62,13 @@
     own_ids = ids[pl.ds(src, 1), :]
     idcol[...] = jnp.transpose(jnp.broadcast_to(own_ids, (128, FW)))
 
-    def picked(f_index, q):
-        col = idcol[pl.ds(pl.multiple_of(f_index * wf, 16), wf), :][:, :1] - feat * raw
-        one_hot = (col == lax.broadcasted_iota(jnp.int32, (wf, raw), 1)).astype(
+    def picked(f_index, r):
+        start = pl.multiple_of(f_index * wf + r * part, 16)
+        col = idcol[pl.ds(start, part), :][:, :1] - feat * raw
+        one_hot = (col == lax.broadcasted_iota(jnp.int32, (part, raw), 1)).astype(
             jnp.float32).astype(jnp.bfloat16)
-        return lax.dot_general(one_hot, acts[0, q * half:(q + 1) * half, :], NT,
+        some = acts[0, pl.ds(pl.multiple_of(early * half, 16), half), :]
+        return lax.dot_general(one_hot, some, NT,
                                preferred_element_type=jnp.float32).astype(jnp.bfloat16)
 
     def remote(a, b, s, r, where):
@@ -96,32 +104,40 @@
     def e_at(p):
         return e_all.at[:, pl.ds(pl.multiple_of(p * rows, 16), rows), :]
 
-    def e_place(j, par):
-        g = lax.rem(group - j + G, G)
-        return (2 * (g // F) + par) * F + lax.rem(g, F)
-
-    def e_copy(j):
-        g = lax.rem(group + j, G)
-        return remote(enc, e_at(plane), e_s.at[j], e_r.at[j],
-                      (2 * (g // F) + parity, tgt, lax.rem(g, F)))
-
-    def e_own_forward():
-        return remote(enc, e_at(plane), ef_s.at[0], ef_r.at[0], (mate, tgt, feat))
-
-    def e_forward(j):
-        place = e_place(j, parity)
-        return remote(e_at(place), e_at(place), ef_s.at[j], ef_r.at[j], (mate, tgt, feat))
-
-    def p_copy(q, j):
-        return remote(pt_send.at[q, j - 1], pt_recv.at[q, j - 1], p_s.at[q, j - 1],
-                      p_r.at[q, j - 1], (src, tgt, lax.rem(feat + j, F)))
+    def place(h, f, par):
+        return (2 * h + par) * F + f
+
+    def e_y(j):
+        return remote(enc, e_at(plane), ey_s.at[j], ey_r.at[j], (src, tgt, lax.rem(feat + j, F)))
+
+    def e_x(i, j, source=None):
+        at = e_at(place(side, lax.rem(feat - j + F, F), parity))
+        return remote(enc if source is None else source, at, ex_s.at[i, j], ex_r.at[i, j],
+                      (2 * lax.rem(side + i, H) + parity, tgt, feat))
+
+    def e_x_out(i, j):
+        if isinstance(j, int) and j == 0:
+            return e_x(i, 0)
+        return e_x(i, j, e_at(place(side, lax.rem(feat - j + F, F), parity)))
+
+    def e_mate(i, j, par, own=False):
+        at = e_at(place(lax.rem(side - i + H, H), lax.rem(feat - j + F, F), par))
+        return remote(enc if own else at, at, ef_s.at[i, j], ef_r.at[i, j], (mate, tgt, feat))
+
+    def p_copy(r, j):
+        return remote(pt_send.at[r, j - 1], pt_recv.at[r, j - 1], p_s.at[r, j - 1],
+                      p_r.at[r, j - 1], (src, tgt, lax.rem(feat + j, F)))
+
+    def z_copy(r, q):
+        at = w_own.at[q, pl.ds(r * part, part), :]
+        return remote(at, at, z_s.at[r], z_r.at[r], (src, tgt + 1 - 2 * early, feat))
 
     def w_at(q, k, f):
         return w_all.at[q, k, pl.ds(pl.multiple_of(f * wf, 16), wf), :]
 
-    def w_copy(q, k, j):
+    def w_copy(n, q, k, j):
         g = lax.rem(group + j, G)
-        return remote(w_own.at[q], w_at(q, k, feat), w_s.at[q, k, j], w_r.at[k, feat],
+        return remote(w_own.at[q], w_at(q, k, feat), w_s.at[n, k, j], w_r.at[k, feat],
                       (2 * (g // F) + q, tgt, lax.rem(g, F)))
 
     def w_arrival(k, f):
@@ -154,67 +170,85 @@
     def _():
         chain(0, chunks)
 
-    for q in range(2):
+    for r in range(pieces):
         for j in range(1, F):
-            pt_send[q, j - 1] = picked(lax.rem(feat + j, F), q)
-            p_copy(q, j).start()
-
-    each(G, lambda j: e_copy(j).start(), 1)
-    e_own_forward().start()
+            pt_send[r, j - 1] = picked(lax.rem(feat + j, F), r)
+            p_copy(r, j).start()
+
+    each(H, lambda i: e_x_out(i, 0).start(), 1)
+    e_mate(0, 0, parity, True).start()
     local = pltpu.make_async_copy(enc, e_at(plane), l_s)
     local.start()
-    for q in range(2):
-        w_own[q] = picked(feat, q)
-    marks = [0, chunks * 4 // 10, chunks * 8 // 10, chunks]
+    for r in range(pieces):
+        w_own[early, r * part:(r + 1) * part] = picked(feat, r)
+    marks = [0, chunks * 3 // 10, chunks * 5 // 10, chunks * 8 // 10, chunks]
 
     def chain_part(n):
         @pl.when(tgt > 0)
         def _():
             chain(marks[n], marks[n + 1])
 
-    for q in range(2):
-        chain_part(q)
-        for j in range(1, F):
-            p_copy(q, j).wait_recv()
-            w_own[q] = w_own[q] + pt_recv[q, j - 1]
+    def mine(k, f):
+        return (src == tgt * K + k) & (feat == f)
+
+    def mates(k, f):
+        return (mate == tgt * K + k) & (feat == f)
+
+    def w_send(n, q):
         for k in range(K):
             def send(j):
-                if_sends(q, k, j, lambda: w_copy(q, k, j).start())
+                if_sends(q, k, j, lambda: w_copy(n, q, k, j).start())
             each(G, send)
 
             @pl.when(src == tgt * K + k)
             def _():
                 w_all[q, k, pl.ds(pl.multiple_of(feat * wf, 16), wf), :] = w_own[q]
 
-    def pass_on(j):
-        e_copy(j).wait_recv()
-        e_forward(j).start()
-
-    each(G, pass_on, 1)
+    def w_pass():
+        for k in range(K):
+            for f in range(F):
+                @pl.when(jnp.logical_not(mine(k, f)))
+                def _():
+                    w_arrival(k, f).wait_recv()
+
+                @pl.when(jnp.logical_not(mates(k, f)))
+                def _():
+                    w_forward(k, f).start()
+
+    chain_part(0)
+    for r in range(pieces):
+        at = slice(r * part, (r + 1) * part)
+        for j in range(1, F):
+            p_copy(r, j).wait_recv()
+            w_own[early, at] = w_own[early, at] + pt_recv[r, j - 1]
+        z_copy(r, early).start()
+    w_send(0, early)
+    each(F, lambda j: e_y(j).start(), 1)
+    chain_part(1)
+
+    def e_turn(j):
+        e_y(j).wait_recv()
+        each(H, lambda i: e_x_out(i, j).start(), 1)
+        e_mate(0, j, parity).start()
+
+    each(F, e_turn, 1)
     chain_part(2)
-
-    def mine(k, f):
-        return (src == tgt * K + k) & (feat == f)
-
-    def mates(k, f):
-        return (mate == tgt * K + k) & (feat == f)
-
-    for k in range(K):
-        for f in range(F):
-            @pl.when(jnp.logical_not(mine(k, f)))
-            def _():
-                w_arrival(k, f).wait_recv()
-
-            @pl.when(jnp.logical_not(mates(k, f)))
-            def _():
-                w_forward(k, f).start()
-
-    e_own_in = lambda j: remote(e_at(e_place(j, 1 - parity)), e_at(e_place(j, 1 - parity)),
-                                ef_s.at[j], ef_r.at[j], (mate, tgt, feat))
-    each(G, lambda j: e_own_in(j).wait_recv())
+    for r in range(pieces):
+        z_copy(r, late).wait_recv()
+    w_send(1, late)
+    pl.when(parity == early)(w_pass)
+
+    def e_far(i, j):
+        e_x(i, j).wait_recv()
+        e_mate(i, j, parity).start()
+
+    each(H, lambda i: each(F, lambda j: e_far(i, j)), 1)
+    chain_part(3)
+    each(H, lambda i: each(F, lambda j: e_mate(i, j, 1 - parity).wait_recv()))
     local.wait()
     for k in range(K):
         out[0, k] = jnp.dot(prefix[k], e_all[k], preferred_element_type=jnp.float32)
+    pl.when(parity == late)(w_pass)
 
     for k in range(K):
         for f in range(F):
@@ -229,16 +263,18 @@
     def _():
         each(chunks, lambda i: chain_copy(i).wait_send())
 
-    for q in range(2):
+    for r in range(pieces):
         for j in range(1, F):
-            p_copy(q, j).wait_send()
+            p_copy(r, j).wait_send()
+        z_copy(r, early).wait_send()
+    for n, q in ((0, early), (1, late)):
         for k in range(K):
             def sent(j):
-                if_sends(q, k, j, lambda: w_copy(q, k, j).wait_send())
+                if_sends(q, k, j, lambda: w_copy(n, q, k, j).wait_send())
             each(G, sent)
-    each(G, lambda j: e_copy(j).wait_send(), 1)
-    e_own_forward().wait_send()
-    each(G, lambda j: e_forward(j).wait_send(), 1)
+    each(F, lambda j: e_y(j).wait_send(), 1)
+    each(H, lambda i: each(F, lambda j: e_x_out(i, j).wait_send()), 1)
+    each(H, lambda i: each(F, lambda j: e_mate(i, j, parity).wait_send()))
     for k in range(K):
         for f in range(F):
             @pl.when(jnp.logical_not(mates(k, f)))
@@ -254,6 +290,8 @@
         FW = window_ids.shape[1]
         _, K, wf, D = decoders.shape
         G = S // 2 * F
+        H = S // 2
+        pieces = 2 if wf % 32 == 0 else 1
         bf = jnp.bfloat16
         dma = pltpu.SemaphoreType.DMA
         chunks = wf // (32 if wf % 32 == 0 else 16)
@@ -265,16 +303,16 @@
             out_specs=vmem,
             scratch_shapes=[
                 pltpu.VMEM((FW, 128), jnp.int32),
-                pltpu.VMEM((2, F - 1, wf, tokens // 2), bf),
-                pltpu.VMEM((2, F - 1, wf, tokens // 2), bf),
+                pltpu.VMEM((pieces, F - 1, wf // pieces, tokens // 2), bf),
+                pltpu.VMEM((pieces, F - 1, wf // pieces, tokens // 2), bf),
                 pltpu.VMEM((2, wf, tokens // 2), bf),
                 pltpu.VMEM((2, K, FW, tokens // 2), bf),
                 pltpu.VMEM((K, D, FW), bf),
                 pltpu.VMEM((wf, D), bf),
                 pltpu.VMEM((wf, D), bf),
                 pltpu.VMEM((K, wf, D), bf),
-                dma((2, F - 1)), dma((2, F - 1)),
-                dma((G,)), dma((G,)), dma((G,)), dma((G,)),
+                dma((pieces, F - 1)), dma((pieces, F - 1)), dma((pieces,)), dma((pieces,)),
+                dma((F,)), dma((F,)), dma((H, F)), dma((H, F)), dma((H, F)), dma((H, F)),
                 dma((2, K, G)), dma((K, F)), dma((K, F)), dma((K, F)),
                 dma((chunks,)), dma((chunks,)), dma(()),
             ],

time: 75.3 us -> 69.5 us (0.923)
  the two profiles are of different devices: /device:TPU:31 before, /device:TPU:29 now
where the time goes in v2:
time: 69.5 us; the launch traced here: 69.3 us
  Pallas kernels  67.2 us (97%)
  local copies, waits for them, and re-layouts  2.09 us (3%)
    pallas_call x1, Pallas kernels, per_device(): pl.pallas_call(functools.partial(kernel, S, T, F), out_shape=jax.ShapeDty...  67.2 us
    unnamed x1, local copies, waits for them, and re-layouts  2.09 us

profile of v2, /device:TPU:29, one launch (start us, length us, event | category | flops | bytes accessed | tf_op | source)
XLA Modules:
  0.0 69.3 jit_solution(9209053556354022377)
XLA Ops:
  0.0 67.2 %shard_map.46 = f32[1,1,320,640]{3,2,1,0:T(8,128)} custom-call(bf16[1,1792,640]{2,1,0:T(8,128)(2,1)} %acts.1, s32[4,640]{1,0:T(4,128)} %ids.1, bf16[1,1,320,2048]{3,2,1,0:T(8,128)(2,1)} %dec.1, bf16[1,256,640]{2,1,0:T(8,128)(2,1)} %enc.1), custom_call_target="tpu_custom_call" | custom-call | tf_op jit(solution)/shard_map/pallas_call | solution.py:299
  67.2 2.1 %copy.6 = f32[1,1,320,640]{3,2,1,0:T(8,128)} copy(f32[1,1,320,640]{3,2,1,0:T(8,128)} %shard_map.46) | data formatting | bytes 1638400

commit v3 on v2

--- a/solution.py
+++ b/solution.py
@@ -37,6 +37,8 @@
     pieces = 2 if wf % 32 == 0 else 1
     part = wf // pieces
     early = lax.rem(tgt, 2)
+    has_in = (tgt > 0) & (src < tgt * K)
+    has_out = (tgt < T - 1) & (src < (tgt + 1) * K)
     late = 1 - early
     H = S // 2
     side = src // 2
@@ -84,7 +86,7 @@
         def step(i, carry):
             at = pl.ds(pl.multiple_of(i * chunk, 16), chunk)
 
-            @pl.when(tgt > 0)
+            @pl.when(has_in)
             def _():
                 chain_copy(i).wait_recv()
 
@@ -94,7 +96,7 @@
                 live = (tgt * K + k >= src).astype(jnp.float32)
                 total = total + dec[0, k, at, :].astype(jnp.float32) * live
 
-            @pl.when(tgt < T - 1)
+            @pl.when(has_out)
             def _():
                 ch_send[at, :] = total.astype(jnp.bfloat16)
                 chain_copy(i).start()
@@ -159,14 +161,14 @@
         else:
             pl.when(owner & ((j > 0) | (parity != q)))(fn)
 
-    @pl.when(tgt == 0)
+    @pl.when(jnp.logical_not(has_in))
     def _():
         ch_recv[...] = jnp.zeros_like(ch_recv)
 
     pl.semaphore_wait(barrier, S * F - 1 + (tgt > 0).astype(jnp.int32)
                       + (tgt < T - 1).astype(jnp.int32))
 
-    @pl.when(tgt == 0)
+    @pl.when(jnp.logical_not(has_in))
     def _():
         chain(0, chunks)
 
@@ -184,7 +186,7 @@
     marks = [0, chunks * 3 // 10, chunks * 5 // 10, chunks * 8 // 10, chunks]
 
     def chain_part(n):
-        @pl.when(tgt > 0)
+        @pl.when(has_in)
         def _():
             chain(marks[n], marks[n + 1])
 
@@ -259,7 +261,7 @@
         gram += lax.dot_general(w_own[1], w_all[1, k], NT, preferred_element_type=jnp.float32)
         out[0, k] = out[0, k] * (gram / tokens)
 
-    @pl.when(tgt < T - 1)
+    @pl.when(has_out)
     def _():
         each(chunks, lambda i: chain_copy(i).wait_send())
 
@@ -298,7 +300,7 @@
         vmem = pl.BlockSpec(memory_space=pltpu.VMEM)
         return pl.pallas_call(
             functools.partial(kernel, S, T, F),
-            out_shape=jax.ShapeDtypeStruct((1, K, wf, FW), jnp.float32),
+            out_shape=pltpu.VMEM((1, K, wf, FW), jnp.float32),
             in_specs=[vmem] * 4,
             out_specs=vmem,
             scratch_shapes=[

time: 69.5 us -> 58.9 us (0.85)
  Pallas kernels: 67.2 us -> 57.6 us
  local copies, waits for them, and re-layouts: 2.09 us -> 0.89 us
    pallas_call x1, Pallas kernels: 67.2 us -> 57.6 us  [per_device(): pl.pallas_call(functools.partial(kernel, S, T, F), out_shape=pltpu.VMEM((...]
    unnamed x1, local copies, waits for them, and re-layouts: 2.09 us -> 0.89 us
where the time goes in v3:
time: 58.9 us; the launch traced here: 58.5 us
  Pallas kernels  57.6 us (98%)
  local copies, waits for them, and re-layouts  0.89 us (2%)
    pallas_call x1, Pallas kernels, per_device(): pl.pallas_call(functools.partial(kernel, S, T, F), out_shape=pltpu.VMEM((...  57.6 us

profile of v3, /device:TPU:29, one launch (start us, length us, event | category | flops | bytes accessed | tf_op | source)
XLA Modules:
  0.0 58.5 jit_solution(14439370831308488678)
XLA Ops:
  0.0 57.6 %shard_map.46 = f32[1,1,320,640]{3,2,1,0:T(8,128)S(1)} custom-call(bf16[1,1792,640]{2,1,0:T(8,128)(2,1)} %acts.1, s32[4,640]{1,0:T(4,128)} %ids.1, bf16[1,1,320,2048]{3,2,1,0:T(8,128)(2,1)} %dec.1, bf16[1,256,640]{2,1,0:T(8,128)(2,1)} %enc.1), custom_call_target="tpu_custom_call" | custom-call | tf_op jit(solution)/shard_map/pallas_call | solution.py:301
  57.6 0.9 %copy.6 = f32[1,1,320,640]{3,2,1,0:T(8,128)} copy(f32[1,1,320,640]{3,2,1,0:T(8,128)S(1)} %shard_map.46) | data formatting | bytes 1638400

commit v4 on v3

--- a/solution.py
+++ b/solution.py
@@ -134,25 +134,27 @@
         at = w_own.at[q, pl.ds(r * part, part), :]
         return remote(at, at, z_s.at[r], z_r.at[r], (src, tgt + 1 - 2 * early, feat))
 
-    def w_at(q, k, f):
-        return w_all.at[q, k, pl.ds(pl.multiple_of(f * wf, 16), wf), :]
-
-    def w_copy(n, q, k, j):
+    def w_at(r, q, k, f):
+        return w_all.at[q, k, pl.ds(pl.multiple_of(f * wf + r * part, 16), part), :]
+
+    def w_copy(n, r, q, k, j):
         g = lax.rem(group + j, G)
-        return remote(w_own.at[q], w_at(q, k, feat), w_s.at[n, k, j], w_r.at[k, feat],
+        return remote(w_own.at[q, pl.ds(r * part, part), :], w_at(r, q, k, feat),
+                      w_s.at[n, r, k, j], w_r.at[r, k, feat],
                       (2 * (g // F) + q, tgt, lax.rem(g, F)))
 
-    def w_arrival(k, f):
-        return remote(w_own.at[0], w_at(parity, k, f), w_s.at[0, k, 0], w_r.at[k, f],
-                      (mate, tgt, feat))
-
-    def w_forward(k, f):
-        return remote(w_at(parity, k, f), w_at(parity, k, f), wf_s.at[k, f], wf_r.at[k, f],
-                      (mate, tgt, feat))
-
-    def w_forward_in(k, f):
-        other = w_at(1 - parity, k, f)
-        return remote(other, other, wf_s.at[k, f], wf_r.at[k, f], (mate, tgt, feat))
+    def w_move(r, k, f, par, s, d):
+        at = w_at(r, par, k, f)
+        return remote(at, at, s.at[r, k, f], d.at[r, k, f], (mate, tgt, feat))
+
+    def w_arrival(r, k, f):
+        return w_move(r, k, f, parity, wf_s, w_r)
+
+    def w_forward(r, k, f):
+        return w_move(r, k, f, parity, wf_s, wf_r)
+
+    def w_forward_in(r, k, f):
+        return w_move(r, k, f, 1 - parity, wf_s, wf_r)
 
     def if_sends(q, k, j, fn):
         owner = src == tgt * K + k
@@ -165,6 +167,10 @@
     def _():
         ch_recv[...] = jnp.zeros_like(ch_recv)
 
+    @pl.when(has_in & (tgt == T - 1))
+    def _():
+        out[...] = jnp.zeros_like(out)
+
     pl.semaphore_wait(barrier, S * F - 1 + (tgt > 0).astype(jnp.int32)
                       + (tgt < T - 1).astype(jnp.int32))
 
@@ -186,7 +192,7 @@
     marks = [0, chunks * 3 // 10, chunks * 5 // 10, chunks * 8 // 10, chunks]
 
     def chain_part(n):
-        @pl.when(has_in)
+        @pl.when(has_in & (tgt < T - 1))
         def _():
             chain(marks[n], marks[n + 1])
 
@@ -196,26 +202,28 @@
     def mates(k, f):
         return (mate == tgt * K + k) & (feat == f)
 
-    def w_send(n, q):
+    def w_send(n, r, q):
         for k in range(K):
             def send(j):
-                if_sends(q, k, j, lambda: w_copy(n, q, k, j).start())
+                if_sends(q, k, j, lambda: w_copy(n, r, q, k, j).start())
             each(G, send)
 
             @pl.when(src == tgt * K + k)
             def _():
-                w_all[q, k, pl.ds(pl.multiple_of(feat * wf, 16), wf), :] = w_own[q]
+                w_all[q, k, pl.ds(pl.multiple_of(feat * wf + r * part, 16), part), :] = (
+                    w_own[q, r * part:(r + 1) * part])
 
     def w_pass():
-        for k in range(K):
-            for f in range(F):
-                @pl.when(jnp.logical_not(mine(k, f)))
-                def _():
-                    w_arrival(k, f).wait_recv()
-
-                @pl.when(jnp.logical_not(mates(k, f)))
-                def _():
-                    w_forward(k, f).start()
+        for r in range(pieces):
+            for k in range(K):
+                for f in range(F):
+                    @pl.when(jnp.logical_not(mine(k, f)))
+                    def _():
+                        w_arrival(r, k, f).wait_recv()
+
+                    @pl.when(jnp.logical_not(mates(k, f)))
+                    def _():
+                        w_forward(r, k, f).start()
 
     chain_part(0)
     for r in range(pieces):
@@ -224,7 +232,7 @@
             p_copy(r, j).wait_recv()
             w_own[early, at] = w_own[early, at] + pt_recv[r, j - 1]
         z_copy(r, early).start()
-    w_send(0, early)
+        w_send(0, r, early)
     each(F, lambda j: e_y(j).start(), 1)
     chain_part(1)
 
@@ -237,7 +245,7 @@
     chain_part(2)
     for r in range(pieces):
         z_copy(r, late).wait_recv()
-    w_send(1, late)
+        w_send(1, r, late)
     pl.when(parity == early)(w_pass)
 
     def e_far(i, j):
@@ -246,20 +254,37 @@
 
     each(H, lambda i: each(F, lambda j: e_far(i, j)), 1)
     chain_part(3)
+
     each(H, lambda i: each(F, lambda j: e_mate(i, j, 1 - parity).wait_recv()))
     local.wait()
-    for k in range(K):
-        out[0, k] = jnp.dot(prefix[k], e_all[k], preferred_element_type=jnp.float32)
+    ends = has_in & (tgt == T - 1)
+
+    def virtual(k):
+        return jnp.dot(prefix[k], e_all[k], preferred_element_type=jnp.float32)
+
+    @pl.when(jnp.logical_not(ends))
+    def _():
+        for k in range(K):
+            out[0, k] = virtual(k)
+
     pl.when(parity == late)(w_pass)
 
     for k in range(K):
         for f in range(F):
             @pl.when(jnp.logical_not(mine(k, f)))
             def _():
-                w_forward_in(k, f).wait_recv()
+                for r in range(pieces):
+                    w_forward_in(r, k, f).wait_recv()
         gram = lax.dot_general(w_own[0], w_all[0, k], NT, preferred_element_type=jnp.float32)
         gram += lax.dot_general(w_own[1], w_all[1, k], NT, preferred_element_type=jnp.float32)
-        out[0, k] = out[0, k] * (gram / tokens)
+        gram = gram / tokens
+        out[0, k] = jnp.where(ends, gram, out[0, k] * gram)
+
+    @pl.when(ends)
+    def _():
+        chain(0, chunks)
+        for k in range(K):
+            out[0, k] = virtual(k) * out[0, k]
 
     @pl.when(has_out)
     def _():
@@ -271,9 +296,10 @@
         z_copy(r, early).wait_send()
     for n, q in ((0, early), (1, late)):
         for k in range(K):
-            def sent(j):
-                if_sends(q, k, j, lambda: w_copy(n, q, k, j).wait_send())
-            each(G, sent)
+            for r in range(pieces):
+                def sent(j):
+                    if_sends(q, k, j, lambda: w_copy(n, r, q, k, j).wait_send())
+                each(G, sent)
     each(F, lambda j: e_y(j).wait_send(), 1)
     each(H, lambda i: each(F, lambda j: e_x_out(i, j).wait_send()), 1)
     each(H, lambda i: each(F, lambda j: e_mate(i, j, parity).wait_send()))
@@ -281,7 +307,8 @@
         for f in range(F):
             @pl.when(jnp.logical_not(mates(k, f)))
             def _():
-                w_forward(k, f).wait_send()
+                for r in range(pieces):
+                    w_forward(r, k, f).wait_send()
 
 
 def solution(mesh):
@@ -315,7 +342,8 @@
                 pltpu.VMEM((K, wf, D), bf),
                 dma((pieces, F - 1)), dma((pieces, F - 1)), dma((pieces,)), dma((pieces,)),
                 dma((F,)), dma((F,)), dma((H, F)), dma((H, F)), dma((H, F)), dma((H, F)),
-                dma((2, K, G)), dma((K, F)), dma((K, F)), dma((K, F)),
+                dma((2, pieces, K, G)), dma((pieces, K, F)), dma((pieces, K, F)),
+                dma((pieces, K, F)),
                 dma((chunks,)), dma((chunks,)), dma(()),
             ],
             compiler_params=pltpu.CompilerParams(

time: 58.9 us -> 57.8 us (0.981)
  Pallas kernels: 57.6 us -> 56.7 us
    pallas_call x1, Pallas kernels: 57.6 us -> 56.7 us  [per_device(): pl.pallas_call(functools.partial(kernel, S, T, F), out_shape=pltpu.VMEM((...]
where the time goes in v4:
time: 57.8 us; the launch traced here: 57.6 us
  Pallas kernels  56.7 us (98%)
  local copies, waits for them, and re-layouts  0.89 us (2%)
    pallas_call x1, Pallas kernels, per_device(): pl.pallas_call(functools.partial(kernel, S, T, F), out_shape=pltpu.VMEM((...  56.7 us

profile of v4, /device:TPU:29, one launch (start us, length us, event | category | flops | bytes accessed | tf_op | source)
XLA Modules:
  0.0 57.6 jit_solution(4024529870770417225)
XLA Ops:
  0.0 56.7 %shard_map.46 = f32[1,1,320,640]{3,2,1,0:T(8,128)S(1)} custom-call(bf16[1,1792,640]{2,1,0:T(8,128)(2,1)} %acts.1, s32[4,640]{1,0:T(4,128)} %ids.1, bf16[1,1,320,2048]{3,2,1,0:T(8,128)(2,1)} %dec.1, bf16[1,256,640]{2,1,0:T(8,128)(2,1)} %enc.1), custom_call_target="tpu_custom_call" | custom-call | tf_op jit(solution)/shard_map/pallas_call | solution.py:328
  56.7 0.9 %copy.6 = f32[1,1,320,640]{3,2,1,0:T(8,128)} copy(f32[1,1,320,640]{3,2,1,0:T(8,128)S(1)} %shard_map.46) | data formatting | bytes 1638400
